TPU v7x, 128 devices: a whole 4x4x4 slice. The times are simulated.
128 devices in a mesh: expert: 16 (over y, x), hidden: 8 (over z, core).
Axes of the slice: x: 4, y: 4, z: 4, core: 2. Of those that a mesh axis runs over, the one named last changes fastest.
Arguments:
- tokens: bfloat16 [1024, 7168], P('expert'), may hold values from -6 to 6
- routes: int32 [1024, 8], P('expert'), may hold values from 0 to 31, all different within a row; in each aligned block of 64 rows (0 to 63, 64 to 127, ...) at most 32 rows name the same one
- route_weights: float32 [1024, 8], P('expert'), may hold values from 0.1 to 1
- gate_proj: bfloat16 [32, 7168, 2048], P('expert', None, 'hidden'), may hold values from -0.0625 to 0.0625
- up_proj: bfloat16 [32, 7168, 2048], P('expert', None, 'hidden'), may hold values from -0.0625 to 0.0625
- down_proj: bfloat16 [32, 2048, 7168], P('expert', 'hidden'), may hold values from -0.125 to 0.125
- latents: bfloat16 [1024, 576], P(('expert', 'hidden')), may hold values from -6 to 6
- kv_gain: float32 [512], replicated, may hold values from 0.5 to 1.5
- owners: int32 [1024], P(('expert', 'hidden')), may hold values from 0 to 127, as said below
Outputs:
- moe_out: bfloat16 [1024, 7168], P('expert')
- latent_cache: bfloat16 [2048, 576], P(('expert', 'hidden'))
Inputs may be any that keep to these rules, and one draw needn't show every extreme that they name: `routes`: in each aligned block of 64 tokens (the tokens of one index of the expert axis) no expert is named more than 32 times, a bound that some block reaches; the 8 experts of a token differ. Every owner has 1 to 16 tokens; a quarter of the owners have exactly 16, the others fewer.
All inputs are finite; a program needn't handle non-finite values.
Results may differ from a plain program's by a relative error of at most 0.022.
Values may be sent and summed in bfloat16 or wider, within the bound.
A program may use at most 128 MiB of HBM per device.

v0:
```python
import jax
import jax.numpy as jnp
from jax import lax
from jax.sharding import PartitionSpec as P

KV_RANK = 512
TOP = 8
CAP = 32


def body(tokens, routes, route_weights, gate_proj, up_proj, down_proj, latents, kv_gain, owners):
    n_expert = lax.axis_size("expert")
    n_hidden = lax.axis_size("hidden")
    tok_rows, model_width = tokens.shape
    exp_local = gate_proj.shape[0]
    n_experts = exp_local * n_expert
    slice_rows = CAP // n_hidden
    hidden_index = lax.axis_index("hidden")
    flat_routes = routes.reshape(-1)
    expert_hot = (flat_routes[:, None] == jnp.arange(n_experts, dtype=jnp.int32)[None, :]).astype(
        jnp.int32
    )
    pair_slot = jnp.sum((jnp.cumsum(expert_hot, axis=0) - expert_hot) * expert_hot, axis=1)
    pair_dest = flat_routes * CAP + pair_slot
    matches = pair_dest[None, :] == jnp.arange(n_experts * CAP, dtype=jnp.int32)[:, None]
    selector = jnp.any(matches.reshape(n_experts * CAP, tok_rows, TOP), axis=2).astype(jnp.bfloat16)
    packed = jnp.dot(selector, tokens, preferred_element_type=jnp.float32).astype(jnp.bfloat16)
    packed = packed.reshape(n_expert, exp_local, CAP, model_width)
    arrived = lax.all_to_all(packed, "expert", split_axis=0, concat_axis=0, tiled=True)
    gate_val = jnp.einsum("secd,edf->secf", arrived, gate_proj, preferred_element_type=jnp.float32)
    up_val = jnp.einsum("secd,edf->secf", arrived, up_proj, preferred_element_type=jnp.float32)
    activation = (jax.nn.silu(gate_val) * up_val).astype(jnp.bfloat16)
    down_val = jnp.einsum(
        "secf,efd->secd", activation, down_proj, preferred_element_type=jnp.float32
    )
    partial_value = down_val.astype(jnp.bfloat16)
    summed = lax.psum_scatter(partial_value, "hidden", scatter_dimension=2, tiled=True).astype(
        jnp.float32
    )
    expert_out = summed.astype(jnp.bfloat16)
    returned = lax.all_to_all(expert_out, "expert", split_axis=0, concat_axis=0, tiled=True)
    in_share = (pair_slot // slice_rows == hidden_index).astype(jnp.float32)
    local_row = flat_routes * slice_rows + pair_slot % slice_rows
    picked = returned.reshape(n_experts * slice_rows, model_width)[local_row]
    share_weight = route_weights.reshape(-1) * in_share
    weighted = picked.astype(jnp.float32) * share_weight[:, None]
    local_sum = jnp.sum(weighted.reshape(tok_rows, TOP, model_width), axis=1)
    moe_out = lax.psum(local_sum.astype(jnp.bfloat16), "hidden")
    wide = latents.astype(jnp.float32)
    head_part = wide[:, :KV_RANK]
    scale = lax.rsqrt(jnp.mean(head_part * head_part, axis=1, keepdims=True) + 1e-06)
    normed = jnp.concatenate(
        [head_part * scale * kv_gain[None, :], wide[:, KV_RANK:]], axis=1
    ).astype(jnp.bfloat16)
    my_index = lax.axis_index("expert") * n_hidden + hidden_index
    cache_rows = 2 * latents.shape[0]
    slot_ids = jnp.arange(cache_rows, dtype=jnp.int32)[:, None]
    all_latent, all_owner = (
        lax.all_gather(normed, ("expert", "hidden"), axis=0, tiled=True),
        lax.all_gather(owners, ("expert", "hidden"), axis=0, tiled=True),
    )
    mine = (all_owner == my_index).astype(jnp.int32)
    earlier = jnp.cumsum(mine) - mine
    placing = ((earlier[None, :] == slot_ids) & (mine[None, :] == 1)).astype(jnp.bfloat16)
    latent_cache = jnp.dot(placing, all_latent, preferred_element_type=jnp.float32).astype(
        jnp.bfloat16
    )
    return (moe_out, latent_cache)


def solution(mesh):
    return jax.shard_map(
        body,
        mesh=mesh,
        in_specs=(
            P("expert", None),
            P("expert", None),
            P("expert", None),
            P("expert", None, "hidden"),
            P("expert", None, "hidden"),
            P("expert", "hidden", None),
            P(("expert", "hidden"), None),
            P(),
            P(("expert", "hidden")),
        ),
        out_specs=(P("expert", None), P(("expert", "hidden"), None)),
        check_vma=False,
    )
```

profile of v0, /device:TPU:1, one launch (start us, length us, event | category | flops | bytes accessed | tf_op | source)
XLA Modules:
  0.0 501.4 jit_solution(11077068087052769144)
XLA Ops:
  8.0 0.0 copy-start
  8.0 0.0 reduce-scatter.2.cloned.1.call-start
  8.1 0.8 copy.45
  8.9 0.1 eq.81
  9.0 0.1 eq.77
  9.1 1.2 reduce-window.15
  10.3 0.2 slice_reduce_fusion
  10.5 0.1 fusion.31
  10.6 0.1 reduce_sum.32
  10.7 0.1 copy.48
  10.8 0.7 broadcast_multiply_fusion
  11.5 0.1 copy.49
  11.6 0.7 fusion.8
  12.3 0.0 copy-done
  12.3 7.4 %convolution_convert_fusion = bf16[1024,7168]{1,0:T(8,128)(2,1)} fusion(pred[1024,64]{0,1:T(8,128)(4,1)S(1)} %fusion.8, bf16[64,7168]{1,0:T(8,128)(2,1)S(1)} %copy-done), kind=kOutput, calls=%fused_computation.4 | convolution fusion | flops 946864128 | bytes 15663104 | tf_op jit(solution)/shard_map/dot_general | solution.py:27
  19.7 169.9 %all_to_all.10 = bf16[16,2,32,7168]{3,2,1,0:T(8,128)(2,1)} all-to-all(bf16[16,2,32,7168]{3,2,1,0:T(8,128)(2,1)} %bitcast.66), channel_id=1, replica_groups=mesh['expert'=16,'hidden'=8] {'expert'}, dimensions={0} | all-to-all | bytes 29360128 | tf_op jit(solution)/shard_map/all_to_all | solution.py:29
  189.5 9.3 %fusion.9 = f32[16,2,32,256]{3,2,0,1:T(8,128)S(1)} fusion(bf16[2,7168,256]{2,1,0:T(8,128)(2,1)} %param.12, bf16[16,2,32,7168]{3,2,1,0:T(8,128)(2,1)} %all_to_all.10), kind=kOutput, calls=%fused_computation.14 | convolution fusion | flops 3758096384 | bytes 23068672 | tf_op jit(solution)/shard_map/secd,edf->secf/dot_general | solution.py:30
  198.9 11.4 %fusion.24 = bf16[16,2,32,256]{3,2,0,1:T(8,128)(2,1)S(1)} fusion(bf16[2,7168,256]{2,1,0:T(8,128)(2,1)} %param.13, bf16[16,2,32,7168]{3,2,1,0:T(8,128)(2,1)} %all_to_all.10, f32[16,2,32,256]{3,2,0,1:T(8,128)S(1)} %fusion.9), kind=kOutput, calls=%fused_computation.17 | convolution fusion | flops 3759669248 | bytes 23592960 | tf_op jit(solution)/shard_map/secd,edf->secf/dot_general | solution.py:31
  210.2 10.4 %convert_bitcast_fusion = bf16[16,2,32,7168]{3,2,0,1:T(8,128)(2,1)} fusion(bf16[16,2,32,256]{3,2,0,1:T(8,128)(2,1)S(1)} %fusion.24, bf16[2,256,7168]{2,1,0:T(8,128)(2,1)} %param.14), kind=kOutput, calls=%fused_computation.3 | convolution fusion | flops 3765436416 | bytes 22544384 | tf_op jit(solution)/shard_map/secf,efd->secd/dot_general | solution.py:33
  220.6 16.7 %copy.52 = bf16[16,2,32,7168]{3,0,1,2:T(8,128)(2,1)} copy(bf16[16,2,32,7168]{3,2,0,1:T(8,128)(2,1)} %convert_bitcast_fusion) | data formatting | bytes 29360128 | tf_op jit(solution)/shard_map/convert_element_type | solution.py:36
  237.4 0.0 copy-start.2
  237.4 0.0 copy-start.4
  237.4 0.0 slice-start
  237.4 0.0 reduce-scatter.2.cloned.1.call-update
  237.4 0.0 copy-start.3
  237.4 0.0 copy-start.5
  237.4 0.0 all-gather.2.cloned.1.call-start
  237.5 0.6 copy-done.2
  238.1 0.1 fusion.41
  238.2 0.0 copy-done.4
  238.2 0.1 fusion.43
  238.3 0.0 slice-done
  238.3 0.6 pad_maximum_fusion
  238.9 0.0 all-gather.2.cloned.1.call-update
  238.9 80.8 %reduce-scatter.2.cloned.1.call-done = bf16[16,2,4,7168]{3,0,1,2:T(8,128)(2,1)} async-done(((bf16[16,2,32,7168]{3,0,1,2:T(8,128)(2,1)}), bf16[16,2,4,7168]{3,0,1,2:T(8,128)(2,1)}) %reduce-scatter.2.cloned.1.call-update) | async-done | bytes 1835024 | tf_op jit(solution)/shard_map/reduce_scatter | solution.py:37
  319.7 4.2 copy.53
  323.9 6.6 %all-to-all-start.1 = ((bf16[16,2,4,7168]{3,2,1,0:T(4,128)(2,1)}), bf16[16,2,4,7168]{3,2,1,0:T(4,128)(2,1)}, u32[]{:S(2)}, u32[]{:S(2)}) async-start(bf16[16,2,4,7168]{3,2,1,0:T(4,128)(2,1)} %copy.53), calls=%async_computation.2 | async-start | bytes 3670016 | tf_op jit(solution)/shard_map/all_to_all | solution.py:41
  330.5 0.0 all-reduce.3.cloned.1.call-start
  330.5 0.1 copy.54
  330.6 0.1 mul.79
  330.7 0.0 copy-done.3
  330.7 0.1 copy.55
  330.8 0.0 copy-done.5
  330.8 0.2 dynamic-update-slice
  331.1 82.8 %all-reduce = s32[1024]{0:T(1024)S(1)} all-reduce(s32[1024]{0:T(1024)S(1)} %dynamic-update-slice), channel_id=1, replica_groups=mesh['expert'=16,'hidden'=8] {'expert','hidden'}, use_global_device_ids=true, to_apply=%add | all-reduce | flops 1024 | bytes 8192
  413.9 0.3 reduce-window.19
  414.1 0.1 slice.25
  414.3 0.1 slice_reduce_fusion.1
  414.4 0.0 all-to-all-done.1
  414.4 2.9 reshape.167
  417.4 0.0 copy-start.1
  417.4 7.1 %gather_fusion = bf16[512,7168]{1,0:T(8,128)(2,1)} fusion(bf16[128,7168]{1,0:T(8,128)(2,1)S(1)} %reshape.167, s32[1024]{0:T(1024)S(1)} %pad_clamp_fusion), kind=kCustom, calls=%fused_computation | custom fusion | bytes 14682112 | tf_op jit(solution)/shard_map/gather | solution.py:44
  424.4 9.8 %fusion = bf16[64,7168]{1,0:T(8,128)(2,1)} fusion(bf16[512,7168]{1,0:T(8,128)(2,1)} %gather_fusion, f32[64,8]{1,0:T(8,128)S(1)} %fusion.39), kind=kLoop, calls=%fused_computation.2 | loop fusion | flops 10551296 | bytes 8259584 | tf_op jit(solution)/shard_map/reduce_sum | solution.py:47
  434.3 0.0 all-reduce.3.cloned.1.call-update
  434.3 0.1 convert_subtract_fusion
  434.4 0.0 all-gather.2.cloned.1.call-done
  434.4 2.2 convolution_convert_fusion.1
  436.6 55.2 %all-reduce.3.cloned.1.call-done = bf16[64,7168]{1,0:T(8,128)(2,1)} async-done(((bf16[64,7168]{1,0:T(8,128)(2,1)}), bf16[64,7168]{1,0:T(8,128)(2,1)}) %all-reduce.3.cloned.1.call-update) | async-done | bytes 917520 | tf_op jit(solution)/shard_map/psum | solution.py:48
  491.8 2.2 copy.75
  493.9 0.0 copy-done.1
  (11 shorter events, 0.1 us)
Async XLA Ops:
  8.0 4.3 copy-start
  8.0 311.7 %reduce-scatter.2.cloned.1.call-start = ((), (), s32[]{:S(2)}) async-start(), calls=%async_computation.3 | async-start | bytes 16515072 | tf_op jit(solution)/shard_map/reduce_scatter | solution.py:37
  237.4 0.7 copy-start.2
  237.4 0.8 copy-start.4
  237.4 0.9 slice-start
  237.4 93.3 %copy-start.3 = (f32[64,8]{0,1:T(8,128)S(1)}, f32[64,8]{0,1:T(8,128)}, u32[]{:S(2)}) copy-start(f32[64,8]{0,1:T(8,128)} %param.11) | copy-start | bytes 6148
  237.4 93.4 %copy-start.5 = (s32[8]{0:T(128)S(1)}, s32[8]{0:T(128)}, u32[]{:S(2)}) copy-start(s32[8]{0:T(128)} %param.17) | copy-start | bytes 100
  237.4 197.0 %all-gather.2.cloned.1.call-start = ((), (), s32[]{:S(2)}) async-start(), calls=%async_computation.5 | async-start | bytes 1320960 | tf_op jit(solution)/shard_map/all_gather | solution.py:59
  323.9 90.5 %all-to-all-start.1 = ((bf16[16,2,4,7168]{3,2,1,0:T(4,128)(2,1)}), bf16[16,2,4,7168]{3,2,1,0:T(4,128)(2,1)}, u32[]{:S(2)}, u32[]{:S(2)}) async-start(bf16[16,2,4,7168]{3,2,1,0:T(4,128)(2,1)} %copy.53), calls=%async_computation.2 | async-start | bytes 3670016 | tf_op jit(solution)/shard_map/all_to_all | solution.py:41
  330.5 161.3 %all-reduce.3.cloned.1.call-start = ((), (), s32[]{:S(2)}) async-start(), calls=%async_computation.4 | async-start | bytes 1835008 | tf_op jit(solution)/shard_map/psum | solution.py:48
  417.4 76.6 %copy-start.1 = (bf16[64,7168]{1,0:T(8,128)(2,1)S(1)}, bf16[64,7168]{1,0:T(8,128)(2,1)}, u32[]{:S(2)}) copy-start(bf16[64,7168]{1,0:T(8,128)(2,1)} %param.9) | copy-start | bytes 2752516
Sparse Core Ops, SparseCore 0:
  237.5 82.1 reduce-scatter.1
  434.4 57.3 all-reduce.2
Sparse Core Ops, SparseCore 1:
  241.7 98.8 all-gather.1
where the time goes:
time: 503 us; the launch traced here: 501 us
  blocking collectives  253 us (50%)
  waiting for transfers between devices  136 us (27%)
  matrix products  40.6 us (8%)
  local copies, waits for them, and re-layouts  35.9 us (7%)
  between operations  15.6 us (3%)
  other arithmetic  13.8 us (3%)
  starting transfers between devices  6.69 us (1%)
    all_to_all x1, blocking collectives, body(): lax.all_to_all(packed, 'expert', split_axis=0, concat_axis=0, tiled=True)  170 us
    unnamed x1, blocking collectives  82.8 us
    reduce_scatter x1, waiting for transfers between devices, body(): lax.psum_scatter(partial_value, 'hidden', scatter_dimension=2, tiled=True)  80.8 us
    psum x1, waiting for transfers between devices, body(): moe_out = lax.psum(local_sum.astype(jnp.bfloat16), 'hidden')  55.2 us
    convert_element_type x1, local copies, waits for them, and re-layouts, body(): partial_value = down_val.astype(jnp.bfloat16)  16.7 us
    dot_general x1, matrix products, body(): jnp.einsum('secd,edf->secf', arrived, up_proj, preferred_element_type=jnp...  11.4 us
    dot_general x1, matrix products, body(): jnp.einsum('secf,efd->secd', activation, down_proj, preferred_element_typ...  10.4 us
  transfers between devices with their start and end apart: 4, of which 2 were waited for; matrix products, arithmetic and copies ran while one was open for 6% of the time, Pallas kernels for 0%

commit v1 on v0

v1 whole, which is shorter than its diff:
```python
import functools

import jax
import jax.numpy as jnp
from jax import lax
from jax.experimental import pallas as pl
from jax.experimental.pallas import tpu as pltpu
from jax.sharding import PartitionSpec as P

KV_RANK = 512
TOP = 8
SIDE = 4
ROWS = 64
HALF = 32
QUARTER = 16
WIDE = 7168
PART = 1792
UNITS = 256
N_SEMS = 224
SUBS = ((0, 1024), (1024, 768))

MESH = pl.DeviceIdType.MESH


def moe_kernel(
    tokens,
    routes,
    route_weights,
    gate,
    up,
    down,
    out,
    x,
    w,
    wd,
    acc,
    h,
    gates,
    half_in,
    full_in,
    small_half_in,
    small_full_in,
    own_sum,
    z_in,
    final,
    send_sems,
    recv_sems,
    local_sems,
):
    e = lax.axis_index("expert")
    hid = lax.axis_index("hidden")
    y, xx, z, c = e // SIDE, e % SIDE, hid // 2, hid % 2
    other = 1 - c

    def at(dy=0, dx=0, dz=0, flip=False):
        core = other if flip else c
        return (
            ((y + dy) % SIDE) * SIDE + (xx + dx) % SIDE,
            ((z + dz) % SIDE) * 2 + core,
        )

    x_next, x_prev = at(dx=1), at(dx=3)
    y_next, y_prev = at(dy=1), at(dy=3)
    sibling = at(flip=True)

    keys = {}

    def sem_of(key):
        if key not in keys:
            keys[key] = len(keys)
            assert len(keys) <= N_SEMS
        return keys[key]

    pending = []

    def send(key, src, dst, device):
        i = sem_of(key)
        copy = pltpu.make_async_remote_copy(
            src_ref=src,
            dst_ref=dst,
            send_sem=send_sems.at[i],
            recv_sem=recv_sems.at[i],
            device_id=device,
            device_id_type=MESH,
        )
        copy.start()
        pending.append(copy)

    def arrived(key, landing):
        i = sem_of(key)
        pltpu.make_async_remote_copy(
            src_ref=landing,
            dst_ref=landing,
            send_sem=send_sems.at[i],
            recv_sem=recv_sems.at[i],
            device_id=sibling,
            device_id_type=MESH,
        ).wait_recv()

    def settle():
        for copy in pending:
            copy.wait_send()
        pending.clear()

    locals_ = []

    def local(src, dst):
        copy = pltpu.make_async_copy(src, dst, local_sems.at[len(locals_)])
        copy.start()
        locals_.append(copy)
        return copy

    big = (y, xx)
    small = (xx, y)
    big_next, big_prev = (y_next, x_next), (y_prev, x_prev)
    small_next, small_prev = (x_next, y_next), (x_prev, y_prev)
    STEP = (0, 3, 1, 2)

    def big_at(k, q):
        return (big[k] + STEP[q]) % SIDE

    def small_at(k, r):
        return (small[k] + STEP[r]) % SIDE

    def token_columns(k, half):
        return pl.ds(pl.multiple_of(half * (2 * PART) + k * PART, 128), PART)

    LOW, HIGH = pl.ds(0, HALF), pl.ds(HALF, HALF)
    GLOW, GHIGH = pl.ds(0, HALF // 2), pl.ds(HALF // 2, HALF // 2)

    weight_loads = [local(gate, w.at[pl.ds(0, 2)]), local(up, w.at[pl.ds(2, 2)])]
    token_loads = [
        local(tokens.at[:, token_columns(k, half)], x.at[k, half, big[k], small[k]])
        for k in range(2)
        for half in range(2)
    ]

    chosen = routes[...]
    strength = route_weights[...]
    lanes = lax.broadcasted_iota(jnp.int32, (ROWS, 128), 1)
    dense = jnp.zeros((ROWS, 128), jnp.float32)
    for j in range(TOP):
        dense = dense + jnp.where(lanes % 32 == chosen[:, j : j + 1], strength[:, j : j + 1], 0.0)
    dense_high = dense.astype(jnp.bfloat16).astype(jnp.float32)
    mixed = jnp.where(lanes % 64 < 32, dense_high, dense - dense_high)
    packed = jnp.where(lanes[:HALF] < 64, mixed[:HALF], mixed[HALF:])
    gates[y, xx] = packed.astype(jnp.bfloat16)
    acc[...] = jnp.zeros_like(acc)

    barrier = pltpu.get_barrier_semaphore()
    partners = (x_next, x_prev, y_next, y_prev, at(dz=1), at(dz=2), at(dz=3), sibling)
    for partner in partners:
        pl.semaphore_signal(barrier, inc=1, device_id=partner, device_id_type=MESH)
    pl.semaphore_wait(barrier, len(partners))

    def block(k, q, r):
        return x.at[k, c, big_at(k, q), small_at(k, r)]

    def gate_block(q, r):
        return gates.at[big_at(0, q), small_at(0, r)]

    def send_block(key, k, q, r, device, rows=None):
        ref = block(k, q, r)
        if rows is not None:
            ref = ref.at[rows]
        send(key, ref, ref, device)
        if k == 0:
            ref = gate_block(q, r)
            if rows is not None:
                ref = ref.at[GLOW if rows is LOW else GHIGH]
            send(("g",) + key, ref, ref, device)

    def block_arrived(key, k, q, r, rows=None):
        ref = block(k, q, r)
        if rows is not None:
            ref = ref.at[rows]
        arrived(key, ref)
        if k == 0:
            ref = gate_block(q, r)
            if rows is not None:
                ref = ref.at[GLOW if rows is LOW else GHIGH]
            arrived(("g",) + key, ref)

    def send_own(key, k, device):
        send(key, tokens.at[:, token_columns(k, c)], block(k, 0, 0), device)
        if k == 0:
            send(("g",) + key, gate_block(0, 0), gate_block(0, 0), device)

    def to_sibling(k, q, r):
        send(("c", k, q, r), block(k, q, r), block(k, q, r), sibling)

    def from_sibling(k, q, r):
        arrived(("c", k, q, r), x.at[k, other, big_at(k, q), small_at(k, r)])

    for k in (1, 0):
        send_own(("s1p", k), k, small_next[k])
        send_own(("s1m", k), k, small_prev[k])
    for k in (0, 1):
        send_own(("b1p", k, 0), k, big_next[k])
        send_own(("b1m", k, 0), k, big_prev[k])
    down_half = pl.ds(pl.multiple_of(c * (2 * PART), 128), 2 * PART)
    down_other = pl.ds(pl.multiple_of(other * (2 * PART), 128), 2 * PART)
    send(("wd",), down.at[:, :, down_other], wd.at[c], sibling)
    down_load = local(down.at[:, :, down_half], wd.at[c])

    for k in (0, 1):
        block_arrived(("s1p", k), k, 0, 1)
        send_block(("s2p", k), k, 0, 1, small_next[k], LOW)
        block_arrived(("s1m", k), k, 0, 2)
        send_block(("s2m", k), k, 0, 2, small_prev[k], HIGH)
    for r in (1, 2):
        for k in (0, 1):
            send_block(("b1p", k, r), k, 0, r, big_next[k])
            send_block(("b1m", k, r), k, 0, r, big_prev[k])
            to_sibling(k, 0, r)
    for k in (0, 1):
        block_arrived(("s2p", k), k, 0, 3, LOW)
        block_arrived(("s2m", k), k, 0, 3, HIGH)
        send_block(("b1p", k, 3), k, 0, 3, big_next[k])
        send_block(("b1m", k, 3), k, 0, 3, big_prev[k])
        to_sibling(k, 0, 3)

    def long_step(r):
        for k in (0, 1):
            block_arrived(("b1p", k, r), k, 1, r)
            send_block(("b2p", k, r), k, 1, r, big_next[k], LOW)
            block_arrived(("b1m", k, r), k, 2, r)
            send_block(("b2m", k, r), k, 2, r, big_prev[k], HIGH)
            to_sibling(k, 1, r)
            to_sibling(k, 2, r)

    def far_step(r):
        for k in (0, 1):
            block_arrived(("b2p", k, r), k, 3, r, LOW)
            block_arrived(("b2m", k, r), k, 3, r, HIGH)
            to_sibling(k, 3, r)

    def multiply(k, half, q):
        g = big_at(k, q)
        start = half * (2 * PART) + k * PART

        def one(n, carry):
            left = x[k, half, g].reshape(SIDE * ROWS, PART)
            right = w[n, pl.ds(pl.multiple_of(start, 128), PART), :]
            part = jnp.dot(left, right, preferred_element_type=jnp.float32)
            part = part.reshape(SIDE, ROWS, UNITS)
            if k == 0:
                acc[n, g] += part
            else:
                acc[n, :, g] += part
            return carry

        lax.fori_loop(0, 4, one, 0)

    for copy in weight_loads + token_loads:
        copy.wait()
    long_step(0)
    for k in (0, 1):
        multiply(k, c, 0)
    long_step(1)
    for k in (0, 1):
        for r in (1, 2, 3):
            from_sibling(k, 0, r)
        multiply(k, other, 0)
    long_step(2)
    long_step(3)
    for q in (1, 2):
        for k in (0, 1):
            multiply(k, c, q)
            if q == 1:
                far_step(k)
    for q in (1, 2):
        for k in (0, 1):
            for r in range(SIDE):
                from_sibling(k, q, r)
            multiply(k, other, q)
            if q == 1:
                far_step(2 + k)
    for k in (0, 1):
        multiply(k, c, 3)
    for k in (0, 1):
        for r in range(SIDE):
            from_sibling(k, 3, r)
        multiply(k, other, 3)

    lane = lax.broadcasted_iota(jnp.int32, (128, 2 * UNITS), 0)
    column = lax.broadcasted_iota(jnp.int32, (128, 2 * UNITS), 1)
    wanted = (lane % 32) == (2 * e + column // UNITS)
    pick_low = (wanted & (lane < 64)).astype(jnp.bfloat16)
    pick_high = (wanted & (lane >= 64)).astype(jnp.bfloat16)
    own_units = pl.ds(pl.multiple_of(c * (2 * UNITS), 128), 2 * UNITS)
    other_units = pl.ds(pl.multiple_of(other * (2 * UNITS), 128), 2 * UNITS)

    def activate(q):
        g = big_at(0, q)
        packed_rows = gates[g].reshape(SIDE * HALF, 128)
        low = jnp.dot(packed_rows, pick_low, preferred_element_type=jnp.float32)
        high = jnp.dot(packed_rows, pick_high, preferred_element_type=jnp.float32)
        weight = jnp.concatenate(
            [
                low.reshape(SIDE, HALF, 2 * UNITS),
                high.reshape(SIDE, HALF, 2 * UNITS),
            ],
            axis=1,
        )
        for n in range(2):
            gate_val = acc[n, g]
            value = gate_val / (1.0 + jnp.exp(-gate_val)) * acc[2 + n, g]
            value = value * weight[:, :, n * UNITS : (n + 1) * UNITS]
            where = pl.ds(pl.multiple_of(c * (2 * UNITS) + n * UNITS, 128), UNITS)
            h[g, :, :, where] = value.astype(jnp.bfloat16)
        send(("h", q), h.at[g, :, :, own_units], h.at[g, :, :, own_units], sibling)

    for q in (3, 1, 2, 0):
        activate(q)
    settle()
    down_load.wait()
    arrived(("wd",), wd.at[other])
    for q in (3, 1, 2, 0):
        arrived(("h", q), h.at[big_at(0, q), :, :, other_units])

    FAR, NEXT, PREV, MINE = 0, 1, 2, 3

    def stage(k, slot):
        return x.at[k, 0, slot]

    def partial(k, q, s, slot, add):
        g = big_at(k, q)
        first, width = SUBS[s]

        def one(n, carry):
            start = pl.multiple_of(first + n * 256, 128)
            cols = pl.ds(start, 256)
            left = h[g] if k == 0 else h[:, g]
            right = wd[:, :, :, pl.ds(pl.multiple_of(k * PART + start, 128), 256)]
            part = jnp.dot(
                left.reshape(SIDE * ROWS, 4 * UNITS),
                right.reshape(4 * UNITS, 256),
                preferred_element_type=jnp.float32,
            ).reshape(SIDE, ROWS, 256)
            if add == "low":
                x[k, 0, slot, :, LOW, cols] = (
                    part[:, :HALF] + half_in[k, 0, :, :, cols].astype(jnp.float32)
                ).astype(jnp.bfloat16)
                x[k, 0, slot, :, HIGH, cols] = part[:, HALF:].astype(jnp.bfloat16)
            elif add == "high":
                x[k, 0, slot, :, LOW, cols] = part[:, :HALF].astype(jnp.bfloat16)
                x[k, 0, slot, :, HIGH, cols] = (
                    part[:, HALF:] + half_in[k, 1, :, :, cols].astype(jnp.float32)
                ).astype(jnp.bfloat16)
            else:
                if add == "both":
                    part = part + full_in[k, 0, :, :, cols].astype(jnp.float32)
                    part = part + full_in[k, 1, :, :, cols].astype(jnp.float32)
                x[k, 0, slot, :, :, cols] = part.astype(jnp.bfloat16)
            return carry

        lax.fori_loop(0, width // 256, one, 0)

    def piece(s):
        return pl.ds(*SUBS[s])

    def back_far(k, s):
        partial(k, 3, s, FAR, None)
        cols = piece(s)
        send(
            ("rhp", k, s),
            stage(k, FAR).at[:, LOW, cols],
            half_in.at[k, 0, :, :, cols],
            big_next[k],
        )
        send(
            ("rhm", k, s),
            stage(k, FAR).at[:, HIGH, cols],
            half_in.at[k, 1, :, :, cols],
            big_prev[k],
        )

    def back_near(k, s):
        cols = piece(s)
        arrived(("rhp", k, s), half_in.at[k, 0, :, :, cols])
        partial(k, 2, s, NEXT, "low")
        send(("rfp", k, s), stage(k, NEXT).at[:, :, cols], full_in.at[k, 0, :, :, cols], big_next[k])
        arrived(("rhm", k, s), half_in.at[k, 1, :, :, cols])
        partial(k, 1, s, PREV, "high")
        send(("rfm", k, s), stage(k, PREV).at[:, :, cols], full_in.at[k, 1, :, :, cols], big_prev[k])

    def back_mine(k, s):
        cols = piece(s)
        arrived(("rfp", k, s), full_in.at[k, 0, :, :, cols])
        arrived(("rfm", k, s), full_in.at[k, 1, :, :, cols])
        partial(k, 0, s, MINE, "both")
        far = stage(k, MINE).at[small_at(k, 3)]
        send(("thp", k, s), far.at[LOW, cols], small_half_in.at[k, 0, :, cols], small_next[k])
        send(("thm", k, s), far.at[HIGH, cols], small_half_in.at[k, 1, :, cols], small_prev[k])

    def back_small(k, s):
        cols = piece(s)
        arrived(("thp", k, s), small_half_in.at[k, 0, :, cols])
        j = small_at(k, 2)
        x[k, 0, MINE, j, LOW, cols] = (
            x[k, 0, MINE, j, LOW, cols].astype(jnp.float32)
            + small_half_in[k, 0, :, cols].astype(jnp.float32)
        ).astype(jnp.bfloat16)
        send(("tfp", k, s), stage(k, MINE).at[j, :, cols], small_full_in.at[k, 0, :, cols], small_next[k])
        arrived(("thm", k, s), small_half_in.at[k, 1, :, cols])
        j = small_at(k, 1)
        x[k, 0, MINE, j, HIGH, cols] = (
            x[k, 0, MINE, j, HIGH, cols].astype(jnp.float32)
            + small_half_in[k, 1, :, cols].astype(jnp.float32)
        ).astype(jnp.bfloat16)
        send(("tfm", k, s), stage(k, MINE).at[j, :, cols], small_full_in.at[k, 1, :, cols], small_prev[k])

    def z_rows(d):
        return pl.ds(pl.multiple_of(((z + d) % SIDE) * QUARTER, QUARTER), QUARTER)

    def back_block(k, s):
        cols = piece(s)
        arrived(("tfp", k, s), small_full_in.at[k, 0, :, cols])
        arrived(("tfm", k, s), small_full_in.at[k, 1, :, cols])
        own_sum[k, :, cols] = (
            x[k, 0, MINE, small[k], :, cols].astype(jnp.float32)
            + small_full_in[k, 0, :, cols].astype(jnp.float32)
            + small_full_in[k, 1, :, cols].astype(jnp.float32)
        ).astype(jnp.bfloat16)
        for d in (2, 1, 3):
            send(
                ("z", k, s, d),
                own_sum.at[k, z_rows(d), cols],
                z_in.at[k, d - 1, :, cols],
                at(dz=d),
            )

    def back_z(k, s):
        cols = piece(s)
        for d in (1, 2, 3):
            arrived(("z", k, s, d), z_in.at[k, d - 1, :, cols])
        total = own_sum[k, z_rows(0), cols].astype(jnp.float32)
        for d in (1, 2, 3):
            total = total + z_in[k, d - 1, :, cols].astype(jnp.float32)
        final[k, z_rows(0), cols] = total.astype(jnp.bfloat16)
        for d in (2, 1, 3):
            mine = final.at[k, z_rows(0), cols]
            send(("f", k, s, d), mine, mine, at(dz=d))

    last = []

    def back_out(k, s):
        cols = piece(s)
        for d in (1, 2, 3):
            arrived(("f", k, s, d), final.at[k, z_rows(SIDE - d), cols])
        first, width = SUBS[s]
        where = pl.ds(pl.multiple_of(c * (2 * PART) + k * PART + first, 128), width)
        send(("o", k, s), final.at[k, :, cols], out.at[:, where], sibling)
        last.append(local(final.at[k, :, cols], out.at[:, where]))

    def back_sibling(k, s):
        first, width = SUBS[s]
        where = pl.ds(pl.multiple_of(other * (2 * PART) + k * PART + first, 128), width)
        arrived(("o", k, s), out.at[:, where])

    both = (0, 1)
    for s in both:
        for k in both:
            back_far(k, s)
    for s in both:
        for k in both:
            back_near(k, s)
    for k in both:
        back_mine(k, 0)
    for k in both:
        back_small(k, 0)
    for k in both:
        back_block(k, 0)
    for k in both:
        back_z(k, 0)
    for k in both:
        back_mine(k, 1)
    for k in both:
        back_small(k, 1)
    for k in both:
        back_block(k, 1)
    for k in both:
        back_out(k, 0)
    for k in both:
        back_z(k, 1)
    for k in both:
        back_out(k, 1)
    for s in both:
        for k in both:
            back_sibling(k, s)
    for copy in last:
        copy.wait()
    settle()


def moe(tokens, routes, route_weights, gate, up, down):
    bf16 = jnp.bfloat16
    anywhere = pl.BlockSpec(memory_space=pl.ANY)
    vmem = pl.BlockSpec(memory_space=pltpu.VMEM)
    return pl.pallas_call(
        moe_kernel,
        out_shape=jax.ShapeDtypeStruct((ROWS, WIDE), bf16),
        in_specs=[anywhere, vmem, vmem, anywhere, anywhere, anywhere],
        out_specs=anywhere,
        scratch_shapes=[
            pltpu.VMEM((2, 2, SIDE, SIDE, ROWS, PART), bf16),
            pltpu.VMEM((4, WIDE, UNITS), bf16),
            pltpu.VMEM((2, 2, UNITS, 2 * PART), bf16),
            pltpu.VMEM((4, SIDE, SIDE, ROWS, UNITS), jnp.float32),
            pltpu.VMEM((SIDE, SIDE, ROWS, 4 * UNITS), bf16),
            pltpu.VMEM((SIDE, SIDE, HALF, 128), bf16),
            pltpu.VMEM((2, 2, SIDE, HALF, PART), bf16),
            pltpu.VMEM((2, 2, SIDE, ROWS, PART), bf16),
            pltpu.VMEM((2, 2, HALF, PART), bf16),
            pltpu.VMEM((2, 2, ROWS, PART), bf16),
            pltpu.VMEM((2, ROWS, PART), bf16),
            pltpu.VMEM((2, 3, QUARTER, PART), bf16),
            pltpu.VMEM((2, ROWS, PART), bf16),
            pltpu.SemaphoreType.DMA((N_SEMS,)),
            pltpu.SemaphoreType.DMA((N_SEMS,)),
            pltpu.SemaphoreType.DMA((16,)),
        ],
        compiler_params=pltpu.CompilerParams(
            collective_id=0, has_side_effects=True, vmem_limit_bytes=60 << 20
        ),
        cost_estimate=pl.CostEstimate(
            flops=2 * 3 * 1024 * WIDE * 512, bytes_accessed=24 << 20, transcendentals=1 << 19
        ),
        name="moe",
    )(tokens, routes, route_weights, gate, up, down)


def body(tokens, routes, route_weights, gate_proj, up_proj, down_proj, latents, kv_gain, owners):
    n_hidden = lax.axis_size("hidden")
    wide = latents.astype(jnp.float32)
    head_part = wide[:, :KV_RANK]
    scale = lax.rsqrt(jnp.mean(head_part * head_part, axis=1, keepdims=True) + 1e-06)
    marks = jnp.broadcast_to(owners.astype(jnp.float32)[:, None], (owners.shape[0], 64))
    normed = jnp.concatenate(
        [head_part * scale * kv_gain[None, :], wide[:, KV_RANK:], marks], axis=1
    ).astype(jnp.bfloat16)
    all_latent = lax.all_gather(normed, ("expert", "hidden"), axis=0, tiled=True)

    moe_out = moe(tokens, routes, route_weights, gate_proj, up_proj, down_proj)

    my_index = lax.axis_index("expert") * n_hidden + lax.axis_index("hidden")
    cache_rows = 2 * latents.shape[0]
    slot_ids = jnp.arange(cache_rows, dtype=jnp.int32)[:, None]
    all_owner = all_latent[:, latents.shape[1]].astype(jnp.int32)
    mine = (all_owner == my_index).astype(jnp.int32)
    earlier = jnp.cumsum(mine) - mine
    placing = ((earlier[None, :] == slot_ids) & (mine[None, :] == 1)).astype(jnp.bfloat16)
    latent_cache = jnp.dot(
        placing, all_latent[:, : latents.shape[1]], preferred_element_type=jnp.float32
    ).astype(jnp.bfloat16)
    return (moe_out, latent_cache)


def solution(mesh):
    return jax.shard_map(
        body,
        mesh=mesh,
        in_specs=(
            P("expert", None),
            P("expert", None),
            P("expert", None),
            P("expert", None, "hidden"),
            P("expert", None, "hidden"),
            P("expert", "hidden", None),
            P(("expert", "hidden"), None),
            P(),
            P(("expert", "hidden")),
        ),
        out_specs=(P("expert", None), P(("expert", "hidden"), None)),
        check_vma=False,
    )
```

time: 503 us -> 159 us (0.32)
  blocking collectives: 253 us -> 0 us
  waiting for transfers between devices: 136 us -> 0.04 us
  Pallas kernels: 0 us -> 133 us
  matrix products: 40.6 us -> 2.21 us
  local copies, waits for them, and re-layouts: 35.9 us -> 4.63 us
  other arithmetic: 13.8 us -> 4.65 us
  starting transfers between devices: 6.69 us -> 0.04 us
    all_to_all x1 -> x0, blocking collectives: 170 us -> none  [body(): lax.all_to_all(packed, 'expert', split_axis=0, concat_axis=0, tiled=True)]
    pallas_call x0 -> x1, Pallas kernels: none -> 133 us  [moe(): pl.pallas_call(moe_kernel, out_shape=jax.ShapeDtypeStruct((ROWS, WIDE), b...]
    unnamed x1 -> x0, blocking collectives: 82.8 us -> none
    reduce_scatter x1 -> x0, waiting for transfers between devices: 80.8 us -> none  [body(): lax.psum_scatter(partial_value, 'hidden', scatter_dimension=2, tiled=True)]
    psum x1 -> x0, waiting for transfers between devices: 55.2 us -> none  [body(): moe_out = lax.psum(local_sum.astype(jnp.bfloat16), 'hidden')]
    dot_general x5 -> x1, matrix products: 40.6 us -> 2.21 us  [body(): jnp.dot(placing, all_latent[:, :latents.shape[1]], preferred_element_type...]
    convert_element_type x1 -> x0, local copies, waits for them, and re-layouts: 16.7 us -> none  [body(): partial_value = down_val.astype(jnp.bfloat16)]
    reduce_sum x2 -> x0, other arithmetic: 9.94 us -> none  [the longest x1 9.83 us: body(): local_sum = jnp.sum(weighted.reshape(tok_rows, TOP, model_width), axis=1)]
  transfers between devices with their start and end apart: 4 -> 1, of which waited for: 2 -> 0; matrix products, arithmetic and copies ran while one was open for 6% -> 2% of each run, Pallas kernels for 0% -> 84%
where the time goes in v1:
time: 159 us
  Pallas kernels  133 us (84%)
  between operations  14.1 us (9%)
  other arithmetic  4.65 us (3%)
  local copies, waits for them, and re-layouts  4.63 us (3%)
  matrix products  2.21 us (1%)
    pallas_call x1, Pallas kernels, moe(): pl.pallas_call(moe_kernel, out_shape=jax.ShapeDtypeStruct((ROWS, WIDE), b...  133 us
    unnamed x5, local copies, waits for them, and re-layouts  3.68 us
  transfers between devices with their start and end apart: 1, of which 0 were waited for; matrix products, arithmetic and copies ran while one was open for 2% of the time, Pallas kernels for 84%

profile of v1, /device:TPU:1, one launch (start us, length us, event | category | flops | bytes accessed | tf_op | source)
XLA Modules:
  0.0 159.0 jit_solution(7311898537833804914)
XLA Ops:
  7.2 0.0 all-gather.2.cloned.1.call-start
  7.2 0.8 fusion.9
  8.0 0.7 slice.25
  8.7 0.7 convert_convert_fusion
  9.4 0.8 fusion.11
  10.2 0.1 broadcast_in_dim.2
  10.2 0.7 pad_maximum_fusion
  10.9 0.0 all-gather.2.cloned.1.call-update
  10.9 1.4 copy.13.routes
  12.3 1.4 copy.14.route_weights
  13.7 133.4 %moe.1 = bf16[64,7168]{1,0:T(8,128)(2,1)} custom-call(bf16[64,7168]{1,0:T(8,128)(2,1)} %tokens.1, s32[64,8]{1,0:T(8,128)} %copy.13.routes, f32[64,8]{1,0:T(8,128)} %copy.14.route_weights, bf16[2,7168,256]{2,1,0:T(8,128)(2,1)} %gate.1, bf16[2,7168,256]{2,1,0:T(8,128)(2,1)} %up.1, bf16[2,256,7168]{2,1,0:T(8,128)(2,1)} %down.1), custom_call_target="tpu_custom_call" | custom-call | flops 22548578304 | bytes 25165824 | tf_op jit(solution)/shard_map/moe/pallas_call | solution.py:501
  147.1 0.0 copy-start
  147.1 0.0 all-gather.2.cloned.1.call-done
  147.1 1.3 convert_reduce_fusion
  148.5 0.3 reduce-window.9
  148.7 0.1 slice.27
  148.8 0.1 slice_reduce_fusion
  149.0 0.1 bitcast_subtract_fusion
  149.0 2.2 %fusion.2 = bf16[16,576]{1,0:T(8,128)(2,1)} fusion(bf16[1024,640]{1,0:T(8,128)(2,1)} %all-gather.2.cloned.1.call-done, s32[1024]{0:T(1024)S(1)} %bitcast_subtract_fusion, pred[1024]{0:T(1024)(128)(4,1)S(1)} %broadcast_compare_fusion), kind=kOutput, calls=%fused_computation.2 | convolution fusion | flops 18916352 | bytes 1334272 | tf_op jit(solution)/shard_map/dot_general | solution.py:554
  151.2 0.0 copy-done
  151.2 0.9 copy.16
  (3 shorter events, 0.0 us)
Async XLA Ops:
  7.2 139.9 %all-gather.2.cloned.1.call-start = ((), (), s32[]{:S(2)}) async-start(), calls=%async_computation | async-start | bytes 1320960 | tf_op jit(solution)/shard_map/all_gather | solution.py:543
  147.1 4.2 %copy-start = (bf16[64,7168]{1,0:T(8,128)(2,1)S(1)}, bf16[64,7168]{1,0:T(8,128)(2,1)}, u32[]{:S(2)}) copy-start(bf16[64,7168]{1,0:T(8,128)(2,1)} %moe.1) | copy-start | bytes 2752516
Sparse Core Ops, SparseCore 0:
  11.4 68.8 all-gather.1

commit v2 on v1

--- a/solution.py
+++ b/solution.py
@@ -8,6 +8,12 @@
 from jax.sharding import PartitionSpec as P
 
 KV_RANK = 512
+LAT = 576
+LAT_PART = 384
+LAT_COLS = pl.ds(0, LAT_PART)
+SIDE_COLS = 512
+SLOTS = 16
+N_EXPERTS = 32
 TOP = 8
 SIDE = 4
 ROWS = 64
@@ -16,8 +22,10 @@
 WIDE = 7168
 PART = 1792
 UNITS = 256
-N_SEMS = 224
-SUBS = ((0, 1024), (1024, 768))
+N_SEMS = 256
+SUBS = ((0, 768), (768, 512))
+FIRST = 1280
+OWN = 128
 
 MESH = pl.DeviceIdType.MESH
 
@@ -29,13 +37,20 @@
     gate,
     up,
     down,
+    latents,
+    kv_gain,
+    owners,
     out,
+    cache,
     x,
     w,
     wd,
     acc,
     h,
-    gates,
+    normed,
+    side,
+    lat,
+    z_first_in,
     half_in,
     full_in,
     small_half_in,
@@ -126,7 +141,6 @@
         return pl.ds(pl.multiple_of(half * (2 * PART) + k * PART, 128), PART)
 
     LOW, HIGH = pl.ds(0, HALF), pl.ds(HALF, HALF)
-    GLOW, GHIGH = pl.ds(0, HALF // 2), pl.ds(HALF // 2, HALF // 2)
 
     weight_loads = [local(gate, w.at[pl.ds(0, 2)]), local(up, w.at[pl.ds(2, 2)])]
     token_loads = [
@@ -137,14 +151,24 @@
 
     chosen = routes[...]
     strength = route_weights[...]
-    lanes = lax.broadcasted_iota(jnp.int32, (ROWS, 128), 1)
-    dense = jnp.zeros((ROWS, 128), jnp.float32)
+    expert_row = lax.broadcasted_iota(jnp.int32, (N_EXPERTS, ROWS), 0)
+    dense = jnp.zeros((N_EXPERTS, ROWS), jnp.float32)
     for j in range(TOP):
-        dense = dense + jnp.where(lanes % 32 == chosen[:, j : j + 1], strength[:, j : j + 1], 0.0)
+        dense = dense + jnp.where(expert_row == chosen[j : j + 1], strength[j : j + 1], 0.0)
     dense_high = dense.astype(jnp.bfloat16).astype(jnp.float32)
-    mixed = jnp.where(lanes % 64 < 32, dense_high, dense - dense_high)
-    packed = jnp.where(lanes[:HALF] < 64, mixed[:HALF], mixed[HALF:])
-    gates[y, xx] = packed.astype(jnp.bfloat16)
+    packed = jnp.concatenate([dense_high, dense - dense_high], axis=1)
+    packed = jnp.where(c == 0, packed[:QUARTER], packed[QUARTER:])
+
+    head = latents[:, :KV_RANK].astype(jnp.float32)
+    tail = latents[:, KV_RANK:].astype(jnp.float32)
+    scale = lax.rsqrt(jnp.sum(head * head, axis=1, keepdims=True) / KV_RANK + 1e-06)
+    lat_rows = latents.shape[0]
+    row = lax.broadcasted_iota(jnp.int32, (lat_rows, 2 * LAT_PART - LAT), 0)
+    marks = jnp.zeros(row.shape, jnp.float32)
+    for i in range(lat_rows):
+        marks = jnp.where(row == i, owners[i].astype(jnp.float32), marks)
+    normed[0, :, :KV_RANK] = head * scale * kv_gain[...]
+    normed[0, :, KV_RANK:] = jnp.concatenate([tail, marks], axis=1)
     acc[...] = jnp.zeros_like(acc)
 
     barrier = pltpu.get_barrier_semaphore()
@@ -156,35 +180,67 @@
     def block(k, q, r):
         return x.at[k, c, big_at(k, q), small_at(k, r)]
 
-    def gate_block(q, r):
-        return gates.at[big_at(0, q), small_at(0, r)]
-
     def send_block(key, k, q, r, device, rows=None):
         ref = block(k, q, r)
         if rows is not None:
             ref = ref.at[rows]
         send(key, ref, ref, device)
-        if k == 0:
-            ref = gate_block(q, r)
-            if rows is not None:
-                ref = ref.at[GLOW if rows is LOW else GHIGH]
-            send(("g",) + key, ref, ref, device)
 
     def block_arrived(key, k, q, r, rows=None):
         ref = block(k, q, r)
         if rows is not None:
             ref = ref.at[rows]
         arrived(key, ref)
-        if k == 0:
-            ref = gate_block(q, r)
-            if rows is not None:
-                ref = ref.at[GLOW if rows is LOW else GHIGH]
-            arrived(("g",) + key, ref)
 
     def send_own(key, k, device):
         send(key, tokens.at[:, token_columns(k, c)], block(k, 0, 0), device)
-        if k == 0:
-            send(("g",) + key, gate_block(0, 0), gate_block(0, 0), device)
+
+    SIDE_LEFT, SIDE_RIGHT = pl.ds(0, SIDE_COLS // 2), pl.ds(SIDE_COLS // 2, SIDE_COLS // 2)
+
+    def side_ref(dy=0, dx=0):
+        return side.at[c, (y + dy) % SIDE, (xx + dx) % SIDE]
+
+    def side_row(dy=0):
+        return side.at[c, (y + dy) % SIDE]
+
+    def side_one():
+        arrived(("n",), normed.at[1])
+        first = jnp.where(c == 0, normed[0], normed[1])
+        second = jnp.where(c == 0, normed[1], normed[0])
+        pair = jnp.concatenate([first, second], axis=0)
+        pair = jnp.where(c == 0, pair[:, :LAT_PART], pair[:, LAT_PART:])
+        side[c, y, xx] = jnp.concatenate([pair, packed], axis=1).astype(jnp.bfloat16)
+        send(("g1p",), side_ref(), side_ref(), x_next)
+        send(("g1m",), side_ref(), side_ref(), x_prev)
+
+    def side_two():
+        arrived(("g1p",), side_ref(dx=3))
+        ref = side_ref(dx=3).at[:, SIDE_LEFT]
+        send(("g2p",), ref, ref, x_next)
+        arrived(("g1m",), side_ref(dx=1))
+        ref = side_ref(dx=1).at[:, SIDE_RIGHT]
+        send(("g2m",), ref, ref, x_prev)
+
+    def side_three():
+        arrived(("g2p",), side_ref(dx=2).at[:, SIDE_LEFT])
+        arrived(("g2m",), side_ref(dx=2).at[:, SIDE_RIGHT])
+        send(("g3p",), side_row(), side_row(), y_next)
+        send(("g3m",), side_row(), side_row(), y_prev)
+
+    def side_four():
+        arrived(("g3p",), side_row(3))
+        ref = side_row(3).at[:, :, SIDE_LEFT]
+        send(("g4p",), ref, ref, y_next)
+        arrived(("g3m",), side_row(1))
+        ref = side_row(1).at[:, :, SIDE_RIGHT]
+        send(("g4m",), ref, ref, y_prev)
+
+    def side_done():
+        arrived(("g4p",), side_row(2).at[:, :, SIDE_LEFT])
+        arrived(("g4m",), side_row(2).at[:, :, SIDE_RIGHT])
+        send(("gc",), side.at[c], side.at[c], sibling)
+        for d in (2, 1, 3):
+            send(("lz", d), side.at[c, :, :, :, LAT_COLS], lat.at[c, :, :, z], at(dz=d))
 
     def to_sibling(k, q, r):
         send(("c", k, q, r), block(k, q, r), block(k, q, r), sibling)
@@ -192,12 +248,14 @@
     def from_sibling(k, q, r):
         arrived(("c", k, q, r), x.at[k, other, big_at(k, q), small_at(k, r)])
 
+    send(("n",), normed.at[0], normed.at[1], sibling)
     for k in (1, 0):
         send_own(("s1p", k), k, small_next[k])
         send_own(("s1m", k), k, small_prev[k])
     for k in (0, 1):
         send_own(("b1p", k, 0), k, big_next[k])
         send_own(("b1m", k, 0), k, big_prev[k])
+    side_one()
     down_half = pl.ds(pl.multiple_of(c * (2 * PART), 128), 2 * PART)
     down_other = pl.ds(pl.multiple_of(other * (2 * PART), 128), 2 * PART)
     send(("wd",), down.at[:, :, down_other], wd.at[c], sibling)
@@ -219,6 +277,7 @@
         send_block(("b1p", k, 3), k, 0, 3, big_next[k])
         send_block(("b1m", k, 3), k, 0, 3, big_prev[k])
         to_sibling(k, 0, 3)
+    side_two()
 
     def long_step(r):
         for k in (0, 1):
@@ -235,74 +294,85 @@
             block_arrived(("b2m", k, r), k, 3, r, HIGH)
             to_sibling(k, 3, r)
 
-    def multiply(k, half, q):
-        g = big_at(k, q)
+    def multiply(k, half, blocks):
         start = half * (2 * PART) + k * PART
+        places = [(big_at(k, q), small_at(k, r)) for q, r in blocks]
 
         def one(n, carry):
-            left = x[k, half, g].reshape(SIDE * ROWS, PART)
+            left = jnp.concatenate([x[k, half, g, j] for g, j in places], axis=0)
             right = w[n, pl.ds(pl.multiple_of(start, 128), PART), :]
             part = jnp.dot(left, right, preferred_element_type=jnp.float32)
-            part = part.reshape(SIDE, ROWS, UNITS)
-            if k == 0:
-                acc[n, g] += part
-            else:
-                acc[n, :, g] += part
+            for i, (g, j) in enumerate(places):
+                piece = part[i * ROWS : (i + 1) * ROWS]
+                if k == 0:
+                    acc[n, g, j] += piece
+                else:
+                    acc[n, j, g] += piece
             return carry
 
         lax.fori_loop(0, 4, one, 0)
+
+    NEAR_ROW = ((0, 0), (0, 1), (0, 2), (0, 3))
+    EARLY = ((1, 0), (1, 1), (2, 0), (2, 1))
+    LATE = ((1, 2), (1, 3), (2, 2), (2, 3))
+    FAR_ROW = ((3, 0), (3, 1), (3, 2), (3, 3))
+
+    def rest(k, blocks):
+        for q, r in blocks:
+            if (q, r) != (0, 0):
+                from_sibling(k, q, r)
+        multiply(k, other, blocks)
 
     for copy in weight_loads + token_loads:
         copy.wait()
     long_step(0)
     for k in (0, 1):
-        multiply(k, c, 0)
+        multiply(k, c, NEAR_ROW)
+    side_three()
     long_step(1)
     for k in (0, 1):
-        for r in (1, 2, 3):
-            from_sibling(k, 0, r)
-        multiply(k, other, 0)
+        rest(k, NEAR_ROW)
+    for k in (0, 1):
+        multiply(k, c, EARLY)
     long_step(2)
+    for k in (0, 1):
+        rest(k, EARLY)
+    side_four()
     long_step(3)
-    for q in (1, 2):
-        for k in (0, 1):
-            multiply(k, c, q)
-            if q == 1:
-                far_step(k)
-    for q in (1, 2):
-        for k in (0, 1):
-            for r in range(SIDE):
-                from_sibling(k, q, r)
-            multiply(k, other, q)
-            if q == 1:
-                far_step(2 + k)
-    for k in (0, 1):
-        multiply(k, c, 3)
-    for k in (0, 1):
-        for r in range(SIDE):
-            from_sibling(k, 3, r)
-        multiply(k, other, 3)
-
-    lane = lax.broadcasted_iota(jnp.int32, (128, 2 * UNITS), 0)
-    column = lax.broadcasted_iota(jnp.int32, (128, 2 * UNITS), 1)
-    wanted = (lane % 32) == (2 * e + column // UNITS)
-    pick_low = (wanted & (lane < 64)).astype(jnp.bfloat16)
-    pick_high = (wanted & (lane >= 64)).astype(jnp.bfloat16)
+    far_step(0)
+    for k in (0, 1):
+        multiply(k, c, LATE)
+    far_step(1)
+    for k in (0, 1):
+        rest(k, LATE)
+    side_done()
+    far_step(2)
+    far_step(3)
+    for k in (0, 1):
+        multiply(k, c, FAR_ROW)
+    for k in (0, 1):
+        rest(k, FAR_ROW)
+
+    expert = lax.broadcasted_iota(jnp.int32, (N_EXPERTS, 2 * UNITS), 0)
+    column = lax.broadcasted_iota(jnp.int32, (N_EXPERTS, 2 * UNITS), 1)
+    pick = (expert == 2 * e + column // UNITS).astype(jnp.bfloat16)
+    arrived(("gc",), side.at[other])
     own_units = pl.ds(pl.multiple_of(c * (2 * UNITS), 128), 2 * UNITS)
     other_units = pl.ds(pl.multiple_of(other * (2 * UNITS), 128), 2 * UNITS)
 
     def activate(q):
         g = big_at(0, q)
-        packed_rows = gates[g].reshape(SIDE * HALF, 128)
-        low = jnp.dot(packed_rows, pick_low, preferred_element_type=jnp.float32)
-        high = jnp.dot(packed_rows, pick_high, preferred_element_type=jnp.float32)
-        weight = jnp.concatenate(
-            [
-                low.reshape(SIDE, HALF, 2 * UNITS),
-                high.reshape(SIDE, HALF, 2 * UNITS),
-            ],
-            axis=1,
-        )
+        weights = []
+        for j in range(SIDE):
+            halves = [side[core, g, j, :, 3 * 128 :] for core in range(2)]
+            both_parts = lax.dot_general(
+                jnp.concatenate(halves, axis=0),
+                pick,
+                (((0,), (0,)), ((), ())),
+                preferred_element_type=jnp.float32,
+            )
+            weights.append((both_parts[:ROWS] + both_parts[ROWS:])[None])
+        weight = jnp.concatenate(weights, axis=0)
         for n in range(2):
             gate_val = acc[n, g]
             value = gate_val / (1.0 + jnp.exp(-gate_val)) * acc[2 + n, g]
@@ -324,9 +394,8 @@
     def stage(k, slot):
         return x.at[k, 0, slot]
 
-    def partial(k, q, s, slot, add):
+    def partial(k, q, first, width, slot, add=None):
         g = big_at(k, q)
-        first, width = SUBS[s]
 
         def one(n, carry):
             start = pl.multiple_of(first + n * 256, 128)
@@ -357,11 +426,43 @@
 
         lax.fori_loop(0, width // 256, one, 0)
 
+    def gather_sum(ref, *others):
+        total = ref[...].astype(jnp.float32)
+        for one in others:
+            total = total + one[...].astype(jnp.float32)
+        ref[...] = total.astype(jnp.bfloat16)
+
+    def own_of(d):
+        return pl.ds(pl.multiple_of(FIRST + OWN * ((z + d) % SIDE), OWN), OWN)
+
     def piece(s):
-        return pl.ds(*SUBS[s])
+        return own_of(0) if s == 2 else pl.ds(*SUBS[s])
+
+    def z_first(k, i, slots, qs):
+        for slot, q in zip(slots, qs):
+            partial(k, q, FIRST, SIDE * OWN, slot)
+        where = pl.ds(slots[0], len(slots))
+        for d in (2, 1, 3):
+            send(
+                ("zq", k, i, d),
+                x.at[k, 0, where, :, :, own_of(d)],
+                z_first_in.at[k, d - 1, where],
+                at(dz=d),
+            )
+
+    def z_first_sum(k, i, slots):
+        where = pl.ds(slots[0], len(slots))
+        for d in (1, 2, 3):
+            arrived(("zq", k, i, d), z_first_in.at[k, d - 1, where])
+        for slot in slots:
+            gather_sum(
+                x.at[k, 0, slot, :, :, own_of(0)],
+                *[z_first_in.at[k, d, slot] for d in range(3)],
+            )
 
     def back_far(k, s):
-        partial(k, 3, s, FAR, None)
+        if s < 2:
+            partial(k, 3, *SUBS[s], FAR)
         cols = piece(s)
         send(
             ("rhp", k, s),
@@ -379,17 +480,30 @@
     def back_near(k, s):
         cols = piece(s)
         arrived(("rhp", k, s), half_in.at[k, 0, :, :, cols])
-        partial(k, 2, s, NEXT, "low")
+        if s < 2:
+            partial(k, 2, *SUBS[s], NEXT, "low")
+        else:
+            gather_sum(stage(k, NEXT).at[:, LOW, cols], half_in.at[k, 0, :, :, cols])
         send(("rfp", k, s), stage(k, NEXT).at[:, :, cols], full_in.at[k, 0, :, :, cols], big_next[k])
         arrived(("rhm", k, s), half_in.at[k, 1, :, :, cols])
-        partial(k, 1, s, PREV, "high")
+        if s < 2:
+            partial(k, 1, *SUBS[s], PREV, "high")
+        else:
+            gather_sum(stage(k, PREV).at[:, HIGH, cols], half_in.at[k, 1, :, :, cols])
         send(("rfm", k, s), stage(k, PREV).at[:, :, cols], full_in.at[k, 1, :, :, cols], big_prev[k])
 
     def back_mine(k, s):
         cols = piece(s)
         arrived(("rfp", k, s), full_in.at[k, 0, :, :, cols])
         arrived(("rfm", k, s), full_in.at[k, 1, :, :, cols])
-        partial(k, 0, s, MINE, "both")
+        if s < 2:
+            partial(k, 0, *SUBS[s], MINE, "both")
+        else:
+            gather_sum(
+                stage(k, MINE).at[:, :, cols],
+                full_in.at[k, 0, :, :, cols],
+                full_in.at[k, 1, :, :, cols],
+            )
         far = stage(k, MINE).at[small_at(k, 3)]
         send(("thp", k, s), far.at[LOW, cols], small_half_in.at[k, 0, :, cols], small_next[k])
         send(("thm", k, s), far.at[HIGH, cols], small_half_in.at[k, 1, :, cols], small_prev[k])
@@ -397,19 +511,13 @@
     def back_small(k, s):
         cols = piece(s)
         arrived(("thp", k, s), small_half_in.at[k, 0, :, cols])
-        j = small_at(k, 2)
-        x[k, 0, MINE, j, LOW, cols] = (
-            x[k, 0, MINE, j, LOW, cols].astype(jnp.float32)
-            + small_half_in[k, 0, :, cols].astype(jnp.float32)
-        ).astype(jnp.bfloat16)
-        send(("tfp", k, s), stage(k, MINE).at[j, :, cols], small_full_in.at[k, 0, :, cols], small_next[k])
+        block = stage(k, MINE).at[small_at(k, 2)]
+        gather_sum(block.at[LOW, cols], small_half_in.at[k, 0, :, cols])
+        send(("tfp", k, s), block.at[:, cols], small_full_in.at[k, 0, :, cols], small_next[k])
         arrived(("thm", k, s), small_half_in.at[k, 1, :, cols])
-        j = small_at(k, 1)
-        x[k, 0, MINE, j, HIGH, cols] = (
-            x[k, 0, MINE, j, HIGH, cols].astype(jnp.float32)
-            + small_half_in[k, 1, :, cols].astype(jnp.float32)
-        ).astype(jnp.bfloat16)
-        send(("tfm", k, s), stage(k, MINE).at[j, :, cols], small_full_in.at[k, 1, :, cols], small_prev[k])
+        block = stage(k, MINE).at[small_at(k, 1)]
+        gather_sum(block.at[HIGH, cols], small_half_in.at[k, 1, :, cols])
+        send(("tfm", k, s), block.at[:, cols], small_full_in.at[k, 1, :, cols], small_prev[k])
 
     def z_rows(d):
         return pl.ds(pl.multiple_of(((z + d) % SIDE) * QUARTER, QUARTER), QUARTER)
@@ -418,11 +526,18 @@
         cols = piece(s)
         arrived(("tfp", k, s), small_full_in.at[k, 0, :, cols])
         arrived(("tfm", k, s), small_full_in.at[k, 1, :, cols])
-        own_sum[k, :, cols] = (
+        total = (
             x[k, 0, MINE, small[k], :, cols].astype(jnp.float32)
             + small_full_in[k, 0, :, cols].astype(jnp.float32)
             + small_full_in[k, 1, :, cols].astype(jnp.float32)
         ).astype(jnp.bfloat16)
+        if s == 2:
+            final[k, :, cols] = total
+            mine = final.at[k, :, cols]
+            for d in (2, 1, 3):
+                send(("f", k, s, d), mine, mine, at(dz=d))
+            return
+        own_sum[k, :, cols] = total
         for d in (2, 1, 3):
             send(
                 ("z", k, s, d),
@@ -445,71 +560,136 @@
 
     last = []
 
+    def columns_of(s):
+        return (FIRST, SIDE * OWN) if s == 2 else SUBS[s]
+
     def back_out(k, s):
-        cols = piece(s)
         for d in (1, 2, 3):
-            arrived(("f", k, s, d), final.at[k, z_rows(SIDE - d), cols])
-        first, width = SUBS[s]
+            if s == 2:
+                landing = final.at[k, :, own_of(SIDE - d)]
+            else:
+                landing = final.at[k, z_rows(SIDE - d), piece(s)]
+            arrived(("f", k, s, d), landing)
+        first, width = columns_of(s)
         where = pl.ds(pl.multiple_of(c * (2 * PART) + k * PART + first, 128), width)
-        send(("o", k, s), final.at[k, :, cols], out.at[:, where], sibling)
-        last.append(local(final.at[k, :, cols], out.at[:, where]))
+        src = final.at[k, :, pl.ds(first, width)]
+        send(("o", k, s), src, out.at[:, where], sibling)
+        last.append(local(src, out.at[:, where]))
 
     def back_sibling(k, s):
-        first, width = SUBS[s]
+        first, width = columns_of(s)
         where = pl.ds(pl.multiple_of(other * (2 * PART) + k * PART + first, 128), width)
         arrived(("o", k, s), out.at[:, where])
 
+    def lat_from_z():
+        for d in (1, 2, 3):
+            arrived(("lz", d), lat.at[c, :, :, (z + SIDE - d) % SIDE])
+        lat[c, :, :, z] = side[c, :, :, :, LAT_COLS]
+        send(("lc",), lat.at[c], lat.at[c], sibling)
+
+    def place_latents():
+        arrived(("lc",), lat.at[other])
+        me = (e * (2 * SIDE) + hid).astype(jnp.float32)
+        seek = lax.broadcasted_iota(jnp.int32, (8, LAT_PART), 1) == LAT_PART - 1
+        seek = seek.astype(jnp.bfloat16)
+        before = lax.broadcasted_iota(jnp.int32, (128, 128), 0)
+        before = before < lax.broadcasted_iota(jnp.int32, (128, 128), 1)
+        before = before.astype(jnp.bfloat16)
+        slot = lax.broadcasted_iota(jnp.int32, (SLOTS, 128), 0).astype(jnp.float32)
+        taken = jnp.zeros((8, 1), jnp.float32)
+        sums = [jnp.zeros((SLOTS, LAT_PART), jnp.float32) for _ in range(2)]
+        for yy in range(SIDE):
+            for pair_of in range(2):
+                rows = [
+                    lat[core, yy, 2 * pair_of : 2 * pair_of + 2].reshape(128, LAT_PART)
+                    for core in range(2)
+                ]
+                owner = lax.dot_general(
+                    seek, rows[1], (((1,), (1,)), ((), ())), preferred_element_type=jnp.float32
+                )
+                mine = (owner == me).astype(jnp.float32)
+                earlier = taken + jnp.dot(
+                    mine.astype(jnp.bfloat16), before, preferred_element_type=jnp.float32
+                )
+                taken = taken + jnp.sum(mine, axis=1, keepdims=True)
+                place = jnp.where(earlier[:1] == slot, mine[:1], 0.0).astype(jnp.bfloat16)
+                for core in range(2):
+                    sums[core] = sums[core] + jnp.dot(
+                        place, rows[core], preferred_element_type=jnp.float32
+                    )
+        cache[:, :LAT_PART] = sums[0].astype(jnp.bfloat16)
+        cache[:, LAT_PART:] = sums[1][:, : LAT - LAT_PART].astype(jnp.bfloat16)
+
     both = (0, 1)
-    for s in both:
+
+    def do(step, s):
         for k in both:
-            back_far(k, s)
-    for s in both:
-        for k in both:
-            back_near(k, s)
+            step(k, s)
+
+    do(back_far, 0)
     for k in both:
-        back_mine(k, 0)
+        z_first(k, 0, (FAR,), (3,))
+    do(back_far, 1)
     for k in both:
-        back_small(k, 0)
+        z_first(k, 1, (NEXT, PREV), (2, 1))
+    do(back_near, 0)
     for k in both:
-        back_block(k, 0)
+        z_first(k, 2, (MINE,), (0,))
+    lat_from_z()
+    do(back_near, 1)
     for k in both:
-        back_z(k, 0)
+        z_first_sum(k, 0, (FAR,))
+    do(back_far, 2)
+    place_latents()
+    do(back_mine, 0)
     for k in both:
-        back_mine(k, 1)
+        z_first_sum(k, 1, (NEXT, PREV))
+    do(back_near, 2)
+    do(back_mine, 1)
+    do(back_small, 0)
     for k in both:
-        back_small(k, 1)
-    for k in both:
-        back_block(k, 1)
-    for k in both:
-        back_out(k, 0)
-    for k in both:
-        back_z(k, 1)
-    for k in both:
-        back_out(k, 1)
-    for s in both:
-        for k in both:
-            back_sibling(k, s)
+        z_first_sum(k, 2, (MINE,))
+    do(back_mine, 2)
+    do(back_small, 1)
+    do(back_block, 0)
+    do(back_small, 2)
+    do(back_block, 1)
+    do(back_z, 0)
+    do(back_block, 2)
+    do(back_z, 1)
+    do(back_out, 0)
+    do(back_out, 2)
+    do(back_out, 1)
+    for s in (0, 2, 1):
+        do(back_sibling, s)
     for copy in last:
         copy.wait()
     settle()
 
 
-def moe(tokens, routes, route_weights, gate, up, down):
+def layer(tokens, routes, route_weights, gate, up, down, latents, kv_gain, owners):
     bf16 = jnp.bfloat16
     anywhere = pl.BlockSpec(memory_space=pl.ANY)
     vmem = pl.BlockSpec(memory_space=pltpu.VMEM)
+    smem = pl.BlockSpec(memory_space=pltpu.SMEM)
     return pl.pallas_call(
         moe_kernel,
-        out_shape=jax.ShapeDtypeStruct((ROWS, WIDE), bf16),
-        in_specs=[anywhere, vmem, vmem, anywhere, anywhere, anywhere],
-        out_specs=anywhere,
+        out_shape=(
+            jax.ShapeDtypeStruct((ROWS, WIDE), bf16),
+            jax.ShapeDtypeStruct((SLOTS, LAT), bf16),
+        ),
+        in_specs=[anywhere, vmem, vmem, anywhere, anywhere, anywhere, vmem, vmem, smem],
+        out_specs=(anywhere, vmem),
         scratch_shapes=[
             pltpu.VMEM((2, 2, SIDE, SIDE, ROWS, PART), bf16),
             pltpu.VMEM((4, WIDE, UNITS), bf16),
             pltpu.VMEM((2, 2, UNITS, 2 * PART), bf16),
             pltpu.VMEM((4, SIDE, SIDE, ROWS, UNITS), jnp.float32),
             pltpu.VMEM((SIDE, SIDE, ROWS, 4 * UNITS), bf16),
-            pltpu.VMEM((SIDE, SIDE, HALF, 128), bf16),
+            pltpu.VMEM((2, 8, 2 * LAT_PART), jnp.float32),
+            pltpu.VMEM((2, SIDE, SIDE, QUARTER, SIDE_COLS), bf16),
+            pltpu.VMEM((2, SIDE, SIDE, SIDE, QUARTER, LAT_PART), bf16),
+            pltpu.VMEM((2, 3, SIDE, SIDE, ROWS, OWN), bf16),
             pltpu.VMEM((2, 2, SIDE, HALF, PART), bf16),
             pltpu.VMEM((2, 2, SIDE, ROWS, PART), bf16),
             pltpu.VMEM((2, 2, HALF, PART), bf16),
@@ -528,33 +708,21 @@
             flops=2 * 3 * 1024 * WIDE * 512, bytes_accessed=24 << 20, transcendentals=1 << 19
         ),
         name="moe",
-    )(tokens, routes, route_weights, gate, up, down)
+    )(tokens, routes, route_weights, gate, up, down, latents, kv_gain, owners)
 
 
 def body(tokens, routes, route_weights, gate_proj, up_proj, down_proj, latents, kv_gain, owners):
-    n_hidden = lax.axis_size("hidden")
-    wide = latents.astype(jnp.float32)
-    head_part = wide[:, :KV_RANK]
-    scale = lax.rsqrt(jnp.mean(head_part * head_part, axis=1, keepdims=True) + 1e-06)
-    marks = jnp.broadcast_to(owners.astype(jnp.float32)[:, None], (owners.shape[0], 64))
-    normed = jnp.concatenate(
-        [head_part * scale * kv_gain[None, :], wide[:, KV_RANK:], marks], axis=1
-    ).astype(jnp.bfloat16)
-    all_latent = lax.all_gather(normed, ("expert", "hidden"), axis=0, tiled=True)
-
-    moe_out = moe(tokens, routes, route_weights, gate_proj, up_proj, down_proj)
-
-    my_index = lax.axis_index("expert") * n_hidden + lax.axis_index("hidden")
-    cache_rows = 2 * latents.shape[0]
-    slot_ids = jnp.arange(cache_rows, dtype=jnp.int32)[:, None]
-    all_owner = all_latent[:, latents.shape[1]].astype(jnp.int32)
-    mine = (all_owner == my_index).astype(jnp.int32)
-    earlier = jnp.cumsum(mine) - mine
-    placing = ((earlier[None, :] == slot_ids) & (mine[None, :] == 1)).astype(jnp.bfloat16)
-    latent_cache = jnp.dot(
-        placing, all_latent[:, : latents.shape[1]], preferred_element_type=jnp.float32
-    ).astype(jnp.bfloat16)
-    return (moe_out, latent_cache)
+    return layer(
+        tokens,
+        routes.T,
+        route_weights.T,
+        gate_proj,
+        up_proj,
+        down_proj,
+        latents,
+        kv_gain.reshape(1, KV_RANK),
+        owners,
+    )
 
 
 def solution(mesh):

time: 159 us -> 123 us (0.77)
  Pallas kernels: 133 us -> 118 us
  between operations: 14.1 us -> 0.64 us
  other arithmetic: 4.65 us -> 0 us
  matrix products: 2.21 us -> 0 us
    pallas_call x1, Pallas kernels: 133 us -> 118 us  [layer(): pl.pallas_call(moe_kernel, out_shape=(jax.ShapeDtypeStruct((ROWS, WIDE),...]
    dot_general x1 -> x0, matrix products: 2.21 us -> none  [body(): jnp.dot(placing, all_latent[:, :latents.shape[1]], preferred_element_type...]
    another operation x4 -> x0, other arithmetic: 1.75 us -> none
    unnamed x5 -> x2, local copies, waits for them, and re-layouts: 3.68 us -> 3.5 us
  transfers between devices with their start and end apart: 1 -> 0, of which waited for: 0 -> 0; matrix products, arithmetic and copies ran while one was open for 2% -> 0% of each run, Pallas kernels for 84% -> 0%
where the time goes in v2:
time: 123 us; the launch traced here: 122 us
  Pallas kernels  118 us (96%)
  local copies, waits for them, and re-layouts  3.5 us (3%)
    pallas_call x1, Pallas kernels, layer(): pl.pallas_call(moe_kernel, out_shape=(jax.ShapeDtypeStruct((ROWS, WIDE),...  118 us
    unnamed x2, local copies, waits for them, and re-layouts  3.5 us

profile of v2, /device:TPU:1, one launch (start us, length us, event | category | flops | bytes accessed | tf_op | source)
XLA Modules:
  0.0 122.3 jit_solution(9117346102433309428)
XLA Ops:
  0.6 118.2 %moe.1 = (bf16[64,7168]{1,0:T(8,128)(2,1)}, bf16[16,576]{1,0:T(8,128)(2,1)}) custom-call(bf16[64,7168]{1,0:T(8,128)(2,1)} %tokens.1, s32[8,64]{1,0:T(8,128)} %bitcast.3, f32[8,64]{1,0:T(8,128)} %bitcast.4, bf16[2,7168,256]{2,1,0:T(8,128)(2,1)} %gate.1, bf16[2,7168,256]{2,1,0:T(8,128)(2,1)} %up.1, bf16[2,256,7168]{2,1,0:T(8,128)(2,1)} %down.1, ...), custom_call_target="tpu_custom_call" | custom-call | flops 22548578304 | bytes 25165824 | tf_op jit(solution)/shard_map/moe/pallas_call | solution.py:675
  118.8 2.2 %copy.13 = bf16[64,7168]{1,0:T(8,128)(2,1)} copy(bf16[64,7168]{1,0:T(8,128)(2,1)} %get-tuple-element.4) | data formatting | bytes 1835008
  121.0 1.3 %copy.14 = bf16[16,576]{1,0:T(8,128)(2,1)} copy(bf16[16,576]{1,0:T(8,128)(2,1)} %get-tuple-element.5) | data formatting | bytes 36864

commit v3 on v2

--- a/solution.py
+++ b/solution.py
@@ -298,8 +298,8 @@
         start = half * (2 * PART) + k * PART
         places = [(big_at(k, q), small_at(k, r)) for q, r in blocks]
 
-        def one(n, carry):
-            left = jnp.concatenate([x[k, half, g, j] for g, j in places], axis=0)
+        left = jnp.concatenate([x[k, half, g, j] for g, j in places], axis=0)
+        for n in range(4):
             right = w[n, pl.ds(pl.multiple_of(start, 128), PART), :]
             part = jnp.dot(left, right, preferred_element_type=jnp.float32)
             for i, (g, j) in enumerate(places):
@@ -308,9 +308,6 @@
                     acc[n, g, j] += piece
                 else:
                     acc[n, j, g] += piece
-            return carry
-
-        lax.fori_loop(0, 4, one, 0)
 
     NEAR_ROW = ((0, 0), (0, 1), (0, 2), (0, 3))
     EARLY = ((1, 0), (1, 1), (2, 0), (2, 1))
@@ -397,16 +394,13 @@
     def partial(k, q, first, width, slot, add=None):
         g = big_at(k, q)
 
-        def one(n, carry):
-            start = pl.multiple_of(first + n * 256, 128)
+        left = h[g] if k == 0 else h[:, g]
+        left = left.reshape(SIDE * ROWS, 4 * UNITS)
+        for start in range(first, first + width, 256):
             cols = pl.ds(start, 256)
-            left = h[g] if k == 0 else h[:, g]
-            right = wd[:, :, :, pl.ds(pl.multiple_of(k * PART + start, 128), 256)]
-            part = jnp.dot(
-                left.reshape(SIDE * ROWS, 4 * UNITS),
-                right.reshape(4 * UNITS, 256),
-                preferred_element_type=jnp.float32,
-            ).reshape(SIDE, ROWS, 256)
+            right = wd[:, :, :, pl.ds(k * PART + start, 256)].reshape(4 * UNITS, 256)
+            part = jnp.dot(left, right, preferred_element_type=jnp.float32)
+            part = part.reshape(SIDE, ROWS, 256)
             if add == "low":
                 x[k, 0, slot, :, LOW, cols] = (
                     part[:, :HALF] + half_in[k, 0, :, :, cols].astype(jnp.float32)
@@ -422,9 +416,6 @@
                     part = part + full_in[k, 0, :, :, cols].astype(jnp.float32)
                     part = part + full_in[k, 1, :, :, cols].astype(jnp.float32)
                 x[k, 0, slot, :, :, cols] = part.astype(jnp.bfloat16)
-            return carry
-
-        lax.fori_loop(0, width // 256, one, 0)
 
     def gather_sum(ref, *others):
         total = ref[...].astype(jnp.float32)

time: 123 us -> 114 us (0.927)
  Pallas kernels: 118 us -> 109 us
    pallas_call x1, Pallas kernels: 118 us -> 109 us  [layer(): pl.pallas_call(moe_kernel, out_shape=(jax.ShapeDtypeStruct((ROWS, WIDE),...]
where the time goes in v3:
time: 114 us; the launch traced here: 113 us
  Pallas kernels  109 us (96%)
  local copies, waits for them, and re-layouts  3.5 us (3%)
    pallas_call x1, Pallas kernels, layer(): pl.pallas_call(moe_kernel, out_shape=(jax.ShapeDtypeStruct((ROWS, WIDE),...  109 us
    unnamed x2, local copies, waits for them, and re-layouts  3.5 us

profile of v3, /device:TPU:1, one launch (start us, length us, event | category | flops | bytes accessed | tf_op | source)
XLA Modules:
  0.0 113.3 jit_solution(11557929003726802323)
XLA Ops:
  0.6 109.2 %moe.1 = (bf16[64,7168]{1,0:T(8,128)(2,1)}, bf16[16,576]{1,0:T(8,128)(2,1)}) custom-call(bf16[64,7168]{1,0:T(8,128)(2,1)} %tokens.1, s32[8,64]{1,0:T(8,128)} %bitcast.3, f32[8,64]{1,0:T(8,128)} %bitcast.4, bf16[2,7168,256]{2,1,0:T(8,128)(2,1)} %gate.1, bf16[2,7168,256]{2,1,0:T(8,128)(2,1)} %up.1, bf16[2,256,7168]{2,1,0:T(8,128)(2,1)} %down.1, ...), custom_call_target="tpu_custom_call" | custom-call | flops 22548578304 | bytes 25165824 | tf_op jit(solution)/shard_map/moe/pallas_call | solution.py:666
  109.8 2.2 %copy.13 = bf16[64,7168]{1,0:T(8,128)(2,1)} copy(bf16[64,7168]{1,0:T(8,128)(2,1)} %get-tuple-element.4) | data formatting | bytes 1835008
  112.0 1.3 %copy.14 = bf16[16,576]{1,0:T(8,128)(2,1)} copy(bf16[16,576]{1,0:T(8,128)(2,1)} %get-tuple-element.5) | data formatting | bytes 36864

commit v4 on v3

--- a/solution.py
+++ b/solution.py
@@ -23,7 +23,7 @@
 PART = 1792
 UNITS = 256
 N_SEMS = 256
-SUBS = ((0, 768), (768, 512))
+SUBS = ((0, 512), (512, 768))
 FIRST = 1280
 OWN = 128
 
@@ -142,6 +142,11 @@
 
     LOW, HIGH = pl.ds(0, HALF), pl.ds(HALF, HALF)
 
+    barrier = pltpu.get_barrier_semaphore()
+    partners = (x_next, x_prev, y_next, y_prev, at(dz=1), at(dz=2), at(dz=3), sibling)
+    for partner in partners:
+        pl.semaphore_signal(barrier, inc=1, device_id=partner, device_id_type=MESH)
+
     weight_loads = [local(gate, w.at[pl.ds(0, 2)]), local(up, w.at[pl.ds(2, 2)])]
     token_loads = [
         local(tokens.at[:, token_columns(k, half)], x.at[k, half, big[k], small[k]])
@@ -169,12 +174,7 @@
         marks = jnp.where(row == i, owners[i].astype(jnp.float32), marks)
     normed[0, :, :KV_RANK] = head * scale * kv_gain[...]
     normed[0, :, KV_RANK:] = jnp.concatenate([tail, marks], axis=1)
-    acc[...] = jnp.zeros_like(acc)
-
-    barrier = pltpu.get_barrier_semaphore()
-    partners = (x_next, x_prev, y_next, y_prev, at(dz=1), at(dz=2), at(dz=3), sibling)
-    for partner in partners:
-        pl.semaphore_signal(barrier, inc=1, device_id=partner, device_id_type=MESH)
+
     pl.semaphore_wait(barrier, len(partners))
 
     def block(k, q, r):
@@ -239,8 +239,6 @@
         arrived(("g4p",), side_row(2).at[:, :, SIDE_LEFT])
         arrived(("g4m",), side_row(2).at[:, :, SIDE_RIGHT])
         send(("gc",), side.at[c], side.at[c], sibling)
-        for d in (2, 1, 3):
-            send(("lz", d), side.at[c, :, :, :, LAT_COLS], lat.at[c, :, :, z], at(dz=d))
 
     def to_sibling(k, q, r):
         send(("c", k, q, r), block(k, q, r), block(k, q, r), sibling)
@@ -260,6 +258,7 @@
     down_other = pl.ds(pl.multiple_of(other * (2 * PART), 128), 2 * PART)
     send(("wd",), down.at[:, :, down_other], wd.at[c], sibling)
     down_load = local(down.at[:, :, down_half], wd.at[c])
+    acc[...] = jnp.zeros_like(acc)
 
     for k in (0, 1):
         block_arrived(("s1p", k), k, 0, 1)
@@ -383,8 +382,9 @@
     settle()
     down_load.wait()
     arrived(("wd",), wd.at[other])
-    for q in (3, 1, 2, 0):
+    def h_from_sibling(q):
         arrived(("h", q), h.at[big_at(0, q), :, :, other_units])
+
 
     FAR, NEXT, PREV, MINE = 0, 1, 2, 3
 
@@ -571,6 +571,10 @@
         first, width = columns_of(s)
         where = pl.ds(pl.multiple_of(other * (2 * PART) + k * PART + first, 128), width)
         arrived(("o", k, s), out.at[:, where])
+
+    def lat_to_z():
+        for d in (2, 1, 3):
+            send(("lz", d), side.at[c, :, :, :, LAT_COLS], lat.at[c, :, :, z], at(dz=d))
 
     def lat_from_z():
         for d in (1, 2, 3):
@@ -617,7 +621,11 @@
         for k in both:
             step(k, s)
 
-    do(back_far, 0)
+    h_from_sibling(3)
+    back_far(0, 0)
+    for q in (1, 2, 0):
+        h_from_sibling(q)
+    back_far(1, 0)
     for k in both:
         z_first(k, 0, (FAR,), (3,))
     do(back_far, 1)
@@ -626,12 +634,11 @@
     do(back_near, 0)
     for k in both:
         z_first(k, 2, (MINE,), (0,))
-    lat_from_z()
+    lat_to_z()
     do(back_near, 1)
     for k in both:
         z_first_sum(k, 0, (FAR,))
     do(back_far, 2)
-    place_latents()
     do(back_mine, 0)
     for k in both:
         z_first_sum(k, 1, (NEXT, PREV))
@@ -644,9 +651,11 @@
     do(back_small, 1)
     do(back_block, 0)
     do(back_small, 2)
+    lat_from_z()
     do(back_block, 1)
     do(back_z, 0)
     do(back_block, 2)
+    place_latents()
     do(back_z, 1)
     do(back_out, 0)
     do(back_out, 2)
@@ -702,8 +711,24 @@
     )(tokens, routes, route_weights, gate, up, down, latents, kv_gain, owners)
 
 
+def hand_over_kernel(moe_in, cache_in, moe_out, cache_out):
+    moe_out[...] = moe_in[...]
+    cache_out[...] = cache_in[...]
+
+
+def hand_over(moe_out, cache):
+    vmem = pl.BlockSpec(memory_space=pltpu.VMEM)
+    return pl.pallas_call(
+        hand_over_kernel,
+        out_shape=tuple(jax.ShapeDtypeStruct(a.shape, a.dtype) for a in (moe_out, cache)),
+        in_specs=[vmem, vmem],
+        out_specs=(vmem, vmem),
+        name="hand_over",
+    )(moe_out, cache)
+
+
 def body(tokens, routes, route_weights, gate_proj, up_proj, down_proj, latents, kv_gain, owners):
-    return layer(
+    moe_out, cache = layer(
         tokens,
         routes.T,
         route_weights.T,
@@ -714,6 +739,7 @@
         kv_gain.reshape(1, KV_RANK),
         owners,
     )
+    return hand_over(moe_out, cache)
 
 
 def solution(mesh):

time: 114 us -> 112 us (0.982)
  local copies, waits for them, and re-layouts: 3.5 us -> 0 us
  Pallas kernels: 109 us -> 111 us
    unnamed x2 -> x0, local copies, waits for them, and re-layouts: 3.5 us -> none
    pallas_call x0 -> x1, Pallas kernels: none -> 2.17 us  [hand_over(): pl.pallas_call(hand_over_kernel, out_shape=tuple((jax.ShapeDtypeStruct(a....]
where the time goes in v4:
time: 112 us
  Pallas kernels  111 us (99%)
    pallas_call x1, Pallas kernels, layer(): pl.pallas_call(moe_kernel, out_shape=(jax.ShapeDtypeStruct((ROWS, WIDE),...  109 us

profile of v4, /device:TPU:1, one launch (start us, length us, event | category | flops | bytes accessed | tf_op | source)
XLA Modules:
  0.0 112.0 jit_solution(15803801501957208940)
XLA Ops:
  0.6 109.2 %moe.1 = (bf16[64,7168]{1,0:T(8,128)(2,1)}, bf16[16,576]{1,0:T(8,128)(2,1)}) custom-call(bf16[64,7168]{1,0:T(8,128)(2,1)} %tokens.1, s32[8,64]{1,0:T(8,128)} %bitcast.3, f32[8,64]{1,0:T(8,128)} %bitcast.4, bf16[2,7168,256]{2,1,0:T(8,128)(2,1)} %gate.1, bf16[2,7168,256]{2,1,0:T(8,128)(2,1)} %up.1, bf16[2,256,7168]{2,1,0:T(8,128)(2,1)} %down.1, ...), custom_call_target="tpu_custom_call" | custom-call | flops 22548578304 | bytes 25165824 | tf_op jit(solution)/shard_map/moe/pallas_call | solution.py:675
  109.9 2.2 %hand_over.1 = (bf16[64,7168]{1,0:T(8,128)(2,1)}, bf16[16,576]{1,0:T(8,128)(2,1)}) custom-call(bf16[64,7168]{1,0:T(8,128)(2,1)} %get-tuple-element.4.moe_in, bf16[16,576]{1,0:T(8,128)(2,1)} %get-tuple-element.5.cache_in), custom_call_target="tpu_custom_call" | custom-call | tf_op jit(solution)/shard_map/hand_over/pallas_call | solution.py:721
